TPU v7x, 128 devices: a whole 4x4x4 slice. The times are simulated.
128 devices in a mesh: dp: 4 (over y), ctx: 32 (over z, x, core).
Axes of the slice: x: 4, y: 4, z: 4, core: 2. Of those that a mesh axis runs over, the one named last changes fastest.
Arguments:
- se_query: bfloat16 [16384, 4096], P(('dp', 'ctx')), parts along dimension 0, may hold values from -6 to 6
- se_key: bfloat16 [16384, 4096], P(('dp', 'ctx')), parts along dimension 0, may hold values from -6 to 6
- se_value: bfloat16 [16384, 4096], P(('dp', 'ctx')), parts along dimension 0, may hold values from -6 to 6
- feature_taps: float32 [3, 3, 4096], replicated, may hold values from -3 to 3
- inner_taps: float32 [7, 4096], replicated, may hold values from -3 to 3
- li_query: bfloat16 [16384, 4096], P(('dp', 'ctx')), parts along dimension 0, may hold values from -6 to 6
- li_key: bfloat16 [16384, 4096], P(('dp', 'ctx')), parts along dimension 0, may hold values from -6 to 6
- long_filter: bfloat16 [4096, 4096], P('ctx'), may hold values from -1 to 1, as said below
Outputs:
- mixed: bfloat16 [16384, 4096], P(('dp', 'ctx')), parts along dimension 0
There are 4 independent parts, one for each index of `dp`. A program takes and returns all parts, laid end to end along the dimension named above; an argument that names none is the same for every part. Nothing has to cross between parts.
Inputs may be any that keep to these rules, and one draw needn't show every extreme that they name: `long_filter`: a causal filter for each channel, rough from lag to lag.
All inputs are finite; a program needn't handle non-finite values.
Results may differ from a plain program's by a relative error of at most 0.011.
Values may be sent and summed in bfloat16 or wider, within the bound.
A program may use at most 128 MiB of HBM per device.

v0:
```python
import functools

import jax
import jax.numpy as jnp
import ml_dtypes
import numpy as np
from jax import lax
from jax.experimental import pallas as pl
from jax.experimental.pallas import tpu as pltpu
from jax.sharding import PartitionSpec as P

MESH = pl.DeviceIdType.MESH
F32, BF16 = jnp.float32, jnp.bfloat16
LANES = 128
HALF = 16


def transform_tables(blocks, block):
    n = 2 * blocks * block
    i, b, m = np.arange(blocks), np.arange(block), np.arange(block)
    first = np.zeros((blocks, 2, blocks))
    last = np.zeros((blocks, blocks, 2))
    ahead = np.zeros((blocks, 2 * block, 2 * block))
    back = np.zeros((blocks, 2 * block, 2 * block))
    first[0, 0] = 1.0
    first[0, 1] = (-1.0) ** i
    last[:, 0, 0] = 1.0
    last[:, 0, 1] = (-1.0) ** i
    h = block // 2
    even = 2 * np.pi * np.outer(2 * blocks * m[:h], b) / n
    odd = 2 * np.pi * np.outer(blocks + 2 * blocks * m[:h], b) / n
    ahead[0, :h, :block] = np.cos(even)
    ahead[0, block : block + h, :block] = -np.sin(even)
    ahead[0, block, :block] = (-1.0) ** b
    ahead[0, h:block, block:] = np.cos(odd)
    ahead[0, block + h :, block:] = -np.sin(odd)
    back[0, :block, :h] = 2 * np.cos(even).T
    back[0, :block, 0] = 1.0
    back[0, :block, block : block + h] = -2 * np.sin(even).T
    back[0, :block, block] = (-1.0) ** b
    back[0, block:, h:block] = 2 * np.cos(odd).T
    back[0, block:, block + h :] = -2 * np.sin(odd).T
    for p in range(1, blocks):
        turn = np.pi * i * p / blocks
        first[p, 0], first[p, 1] = np.cos(turn), -np.sin(turn)
        last[:, p, 0], last[:, p, 1] = np.cos(turn), -np.sin(turn)
        angle = 2 * np.pi * np.outer(p + 2 * blocks * m, b) / n
        c, s = np.cos(angle), np.sin(angle)
        ahead[p] = np.block([[c, s], [-s, c]])
        back[p] = 2 * np.block([[c.T, -s.T], [s.T, c.T]])
    same = np.eye(HALF)
    first = np.kron(first.reshape(2 * blocks, blocks), same)
    last = np.kron(last.reshape(blocks, 2 * blocks), same)
    return [t.astype(ml_dtypes.bfloat16) for t in (first, ahead, back / n, last)]


def kernel(
    n, q_hbm, k_hbm, v_hbm, feature_hbm, inner_hbm, key_hbm, filter_hbm, first_hbm, ahead_hbm, back_hbm, last_hbm,
    out_hbm,
    q, k, v, feature, inner, key, first, ahead, back, last,
    edge_out, edge_in, ext, sig_out, sig_in, filt_in, spec, turned, conv_out,
    local_sem, edge_sem, sig_send, sig_recv, filt_send, filt_recv, conv_send, conv_recv,
):
    me = lax.axis_index("ctx")
    right = lax.rem(me + 1, n)
    rows = q.shape[0]

    def other(s):
        return lax.rem(me + s, n)

    def cols(g):
        return pl.ds(pl.multiple_of(g * LANES, LANES), LANES)

    loads = [
        pltpu.make_async_copy(src, dst, local_sem.at[at])
        for at, (src, dst) in enumerate(
            [
                (k_hbm, k), (v_hbm, v), (q_hbm, q), (feature_hbm, feature), (inner_hbm, inner), (key_hbm, key),
                (first_hbm, first), (ahead_hbm, ahead), (back_hbm, back), (last_hbm, last),
                (filter_hbm.at[:, cols(me)], filt_in.at[me]),
            ]
        )
    ]
    for load in loads:
        load.start()

    barrier = pltpu.get_barrier_semaphore()

    @pl.loop(1, n)
    def _(s):
        pl.semaphore_signal(barrier, inc=1, device_id={"ctx": other(s)}, device_id_type=MESH)

    pl.semaphore_wait(barrier, n - 1)

    def filter_copy(s):
        g = other(s)
        return pltpu.make_async_remote_copy(
            src_ref=filter_hbm.at[:, cols(g)], dst_ref=filt_in.at[me],
            send_sem=filt_send, recv_sem=filt_recv.at[me],
            device_id={"ctx": g}, device_id_type=MESH,
        )

    for load in loads[:4]:
        load.wait()

    row8 = lax.broadcasted_iota(jnp.int32, (8, LANES), 0)

    @pl.loop(0, n)
    def _(g):
        at = cols(g)
        k16 = k[pl.ds(rows - 16, 16), at].astype(F32)
        v16 = v[pl.ds(rows - 16, 16), at].astype(F32)
        q16 = q[pl.ds(rows - 16, 16), at].astype(F32)
        fk = jnp.zeros((8, LANES), F32)
        fv = jnp.zeros((8, LANES), F32)
        for lag in range(3):
            fk = fk + feature[1, pl.ds(lag, 1), at] * k16[8 - lag : 16 - lag]
            fv = fv + feature[2, pl.ds(lag, 1), at] * v16[8 - lag : 16 - lag]
        packed = jnp.where(
            row8 < 2, pltpu.roll(q16[8:], 2, 0),
            jnp.where(row8 < 4, pltpu.roll(k16[8:], 4, 0), pltpu.roll(v16[8:], 6, 0)),
        )
        edge_out[:, at] = jnp.concatenate([fk * fv, packed], axis=0).astype(BF16)

    edge_copy = pltpu.make_async_remote_copy(
        src_ref=edge_out, dst_ref=edge_in, send_sem=edge_sem.at[0], recv_sem=edge_sem.at[1],
        device_id={"ctx": right}, device_id_type=MESH,
    )
    edge_copy.start()

    @pl.loop(1, n)
    def _(s):
        filter_copy(s).start()

    for load in loads[4:6]:
        load.wait()
    edge_copy.wait()

    def signal_block(g):
        at = cols(g)
        edge = jnp.where(me > 0, edge_in[:, at].astype(F32), 0.0)
        packed = edge[8:]
        ext[0, pl.ds(0, 8), :] = pltpu.roll(packed, 6, 0)
        ext[1, pl.ds(0, 8), :] = pltpu.roll(packed, 4, 0)
        ext[2, pl.ds(0, 8), :] = pltpu.roll(packed, 2, 0)
        ext[3, pl.ds(0, 8), :] = edge[:8]
        feats = []
        for stream, ref in enumerate((q, k, v)):
            own = ref[:, at].astype(F32)
            ext[stream, pl.ds(8, rows), :] = own
            total = feature[stream, pl.ds(0, 1), at] * own
            for lag in range(1, 3):
                total = total + feature[stream, pl.ds(lag, 1), at] * ext[stream, pl.ds(8 - lag, rows), :]
            feats.append(total)
        product = feats[1] * feats[2]
        ext[3, pl.ds(8, rows), :] = product
        total = inner[pl.ds(0, 1), at] * product
        for lag in range(1, 7):
            total = total + inner[pl.ds(lag, 1), at] * ext[3, pl.ds(8 - lag, rows), :]
        return (key[:, at].astype(F32) * (feats[0] * total)).astype(BF16)

    def signal_copy(s):
        g = other(s)
        return pltpu.make_async_remote_copy(
            src_ref=sig_out.at[g], dst_ref=sig_in.at[me], send_sem=sig_send, recv_sem=sig_recv.at[me],
            device_id={"ctx": g}, device_id_type=MESH,
        )

    @pl.loop(1, n)
    def _(s):
        sig_out[other(s)] = signal_block(other(s))
        signal_copy(s).start()

    sig_in[me] = signal_block(me)

    def first_step(source, lane):
        @pl.loop(0, rows // 32)
        def _(j):
            at = [pl.ds(pl.multiple_of(j * 32 + 16 * half, 16), 16) for half in range(2)]
            pair = jnp.concatenate([source[:, a, :].reshape(n * 16, LANES) for a in at], axis=1)
            done = jnp.dot(first[...], pair, preferred_element_type=F32).astype(BF16)
            for half in range(2):
                spec[:, at[half], lane : lane + LANES] = done[:, half * LANES : (half + 1) * LANES].reshape(
                    2 * n, 16, LANES
                )

    for load in loads[6:]:
        load.wait()

    def received(landing, sem):
        @pl.loop(1, n)
        def _(s):
            g = other(s)
            pltpu.make_async_copy(landing.at[g], landing.at[g], sem.at[g]).wait()

    received(filt_in, filt_recv)
    first_step(filt_in, LANES)
    received(sig_in, sig_recv)
    first_step(sig_in, 0)

    row = lax.broadcasted_iota(jnp.int32, (rows, LANES), 0)

    @pl.loop(0, n // 4)
    def _(step):
        for u in range(4):
            p = step * 4 + u
            both = jnp.dot(
                ahead[p], spec[pl.ds(2 * p, 2)].reshape(2 * rows, 2 * LANES), preferred_element_type=F32
            )
            xr, hr = both[:rows, :LANES], both[:rows, LANES:]
            xi, hi = both[rows:, :LANES], both[rows:, LANES:]
            real, imag = xr * hr - xi * hi, xr * hi + xi * hr
            if u == 0:
                alone = jnp.logical_and(row == 0, p == 0)
                real = jnp.where(alone, xr * hr, real)
                imag = jnp.where(alone, xi * hi, imag)
            both = jnp.concatenate([real, imag], axis=0).astype(BF16)
            turned[pl.ds(2 * p, 2)] = (
                jnp.dot(back[p], both, preferred_element_type=F32).astype(BF16).reshape(2, rows, LANES)
            )

    def conv_copy(s, part):
        g = other(s)
        at = pl.ds(part * (rows // 2), rows // 2)
        return pltpu.make_async_remote_copy(
            src_ref=conv_out.at[g, at], dst_ref=out_hbm.at[at, cols(me)],
            send_sem=conv_send, recv_sem=conv_recv.at[me],
            device_id={"ctx": g}, device_id_type=MESH,
        )

    for part in range(2):
        @pl.loop(0, rows // 64)
        def _(j):
            at = [pl.ds(pl.multiple_of(part * (rows // 2) + j * 32 + 16 * half, 16), 16) for half in range(2)]
            pair = jnp.concatenate([turned[:, a, :].reshape(2 * n * 16, LANES) for a in at], axis=1)
            done = jnp.dot(last[...], pair, preferred_element_type=F32).astype(BF16)
            for half in range(2):
                conv_out[:, at[half], :] = done[:, half * LANES : (half + 1) * LANES].reshape(n, 16, LANES)

        @pl.loop(1, n)
        def _(s):
            conv_copy(s, part).start()

    own = pltpu.make_async_copy(conv_out.at[me], out_hbm.at[:, cols(me)], local_sem.at[0])
    own.start()
    own.wait()

    @pl.loop(1, n)
    def _(s):
        g = other(s)
        there = out_hbm.at[:, cols(g)]
        pltpu.make_async_copy(there, there, conv_recv.at[g]).wait()

    for ref, sem in ((filt_in, filt_send), (sig_out, sig_send), (conv_out, conv_send)):
        sent = ref.at[pl.ds(0, n - 1)]
        pltpu.make_async_copy(sent, sent, sem).wait()


def solution(mesh):
    n = mesh.shape["ctx"]

    def local(se_query, se_key, se_value, feature_taps, inner_taps, li_query, li_key, long_filter):
        rows, width = se_query.shape
        tables = transform_tables(n, rows)
        block = (n, rows, LANES)
        dma = pltpu.SemaphoreType.DMA
        conv = pl.pallas_call(
            functools.partial(kernel, n),
            out_shape=jax.ShapeDtypeStruct((rows, width), BF16),
            in_specs=[pl.BlockSpec(memory_space=pl.ANY)] * 11,
            out_specs=pl.BlockSpec(memory_space=pl.ANY),
            scratch_shapes=[
                pltpu.VMEM((rows, width), BF16),
                pltpu.VMEM((rows, width), BF16),
                pltpu.VMEM((rows, width), BF16),
                pltpu.VMEM(feature_taps.shape, F32),
                pltpu.VMEM(inner_taps.shape, F32),
                pltpu.VMEM((rows, width), BF16),
                *[pltpu.VMEM(t.shape, BF16) for t in tables],
                pltpu.VMEM((16, width), BF16),
                pltpu.VMEM((16, width), BF16),
                pltpu.VMEM((4, rows + 8, LANES), F32),
                pltpu.VMEM(block, BF16),
                pltpu.VMEM(block, BF16),
                pltpu.VMEM(block, BF16),
                pltpu.VMEM((2 * n, rows, 2 * LANES), BF16),
                pltpu.VMEM((2 * n, rows, LANES), BF16),
                pltpu.VMEM(block, BF16),
                dma((11,)),
                dma((2,)),
                dma,
                dma((n,)),
                dma,
                dma((n,)),
                dma,
                dma((n,)),
            ],
            compiler_params=pltpu.CompilerParams(
                collective_id=0, has_side_effects=True, vmem_limit_bytes=56 * 1024 * 1024
            ),
        )(
            se_query, se_key, se_value, feature_taps, inner_taps, li_key, long_filter,
            *[jnp.asarray(t) for t in tables],
        )
        return (li_query.astype(F32) * conv.astype(F32)).astype(BF16)

    rows_over = P(("dp", "ctx"), None)
    return jax.shard_map(
        local,
        mesh=mesh,
        in_specs=(rows_over, rows_over, rows_over, P(), P(), rows_over, rows_over, P("ctx", None)),
        out_specs=rows_over,
        check_vma=False,
    )
```

profile of v0, /device:TPU:1, one launch (start us, length us, event | category | flops | bytes accessed | tf_op | source)
XLA Modules:
  0.0 62.3 jit_solution(2827402109079702811)
XLA Ops:
  0.0 0.0 copy-start
  0.0 59.9 %shard_map.118 = bf16[128,4096]{1,0:T(8,128)(2,1)} custom-call(bf16[128,4096]{1,0:T(8,128)(2,1)} %q_hbm.1, bf16[128,4096]{1,0:T(8,128)(2,1)} %k_hbm.1, bf16[128,4096]{1,0:T(8,128)(2,1)} %v_hbm.1, f32[3,3,4096]{2,1,0:T(4,128)} %feature_hbm.1, f32[7,4096]{1,0:T(8,128)} %inner_hbm.1, bf16[128,4096]{1,0:T(8,128)(2,1)} %key_hbm.1, bf16[128,4096]{1,0:T(8,128)(2,1)} %filter_hbm.1, ...), custom_call_target="tpu_custom_call" | custom-call | tf_op jit(solution)/shard_map/pallas_call | solution.py:267
  59.9 0.0 copy-done
  59.9 2.4 %multiply_convert_fusion = bf16[128,4096]{1,0:T(8,128)(2,1)} fusion(bf16[128,4096]{1,0:T(8,128)(2,1)} %shard_map.118, bf16[128,4096]{1,0:T(8,128)(2,1)S(1)} %copy-done), kind=kLoop, calls=%fused_computation | loop fusion | flops 2097152 | bytes 3145728 | tf_op jit(solution)/shard_map/convert_element_type | solution.py:305
Async XLA Ops:
  0.0 59.9 %copy-start = (bf16[128,4096]{1,0:T(8,128)(2,1)S(1)}, bf16[128,4096]{1,0:T(8,128)(2,1)}, u32[]{:S(2)}) copy-start(bf16[128,4096]{1,0:T(8,128)(2,1)} %param.17) | copy-start | bytes 3145732
where the time goes:
time: 62.5 us; the launch traced here: 62.3 us
  Pallas kernels  59.9 us (96%)
  other arithmetic  2.45 us (4%)
    pallas_call x1, Pallas kernels, local(): pl.pallas_call(functools.partial(kernel, n), out_shape=jax.ShapeDtypeStru...  59.9 us
    convert_element_type x1, other arithmetic, local(): return (li_query.astype(F32) * conv.astype(F32)).astype(BF16)  2.45 us

commit v1 on v0

v1 whole, which is shorter than its diff:
```python
import functools

import jax
import jax.numpy as jnp
import ml_dtypes
import numpy as np
from jax import lax
from jax.experimental import pallas as pl
from jax.experimental.pallas import tpu as pltpu
from jax.sharding import PartitionSpec as P

MESH = pl.DeviceIdType.MESH
F32, BF16 = jnp.float32, jnp.bfloat16
LANES = 128
HALF = 16
UNROLL = 16


def transform_tables(blocks, block):
    n = 2 * blocks * block
    i, b, m = np.arange(blocks), np.arange(block), np.arange(block)
    first = np.zeros((blocks, 2, blocks))
    last = np.zeros((blocks, blocks, 2))
    ahead = np.zeros((blocks, 2 * block, 2 * block))
    back = np.zeros((blocks, 2 * block, 2 * block))
    first[0, 0] = 1.0
    first[0, 1] = (-1.0) ** i
    last[:, 0, 0] = 1.0
    last[:, 0, 1] = (-1.0) ** i
    h = block // 2
    even = 2 * np.pi * np.outer(2 * blocks * m[:h], b) / n
    odd = 2 * np.pi * np.outer(blocks + 2 * blocks * m[:h], b) / n
    ahead[0, :h, :block] = np.cos(even)
    ahead[0, block : block + h, :block] = -np.sin(even)
    ahead[0, block, :block] = (-1.0) ** b
    ahead[0, h:block, block:] = np.cos(odd)
    ahead[0, block + h :, block:] = -np.sin(odd)
    back[0, :block, :h] = 2 * np.cos(even).T
    back[0, :block, 0] = 1.0
    back[0, :block, block : block + h] = -2 * np.sin(even).T
    back[0, :block, block] = (-1.0) ** b
    back[0, block:, h:block] = 2 * np.cos(odd).T
    back[0, block:, block + h :] = -2 * np.sin(odd).T
    for p in range(1, blocks):
        turn = np.pi * i * p / blocks
        first[p, 0], first[p, 1] = np.cos(turn), -np.sin(turn)
        last[:, p, 0], last[:, p, 1] = np.cos(turn), -np.sin(turn)
        angle = 2 * np.pi * np.outer(p + 2 * blocks * m, b) / n
        c, s = np.cos(angle), np.sin(angle)
        ahead[p] = np.block([[c, s], [-s, c]])
        back[p] = 2 * np.block([[c.T, -s.T], [s.T, c.T]])
    same = np.eye(HALF)
    first = np.kron(first.reshape(2 * blocks, blocks), same)
    last = np.kron(last.reshape(blocks, 2 * blocks), same)
    return [t.astype(ml_dtypes.bfloat16) for t in (first, ahead, back / n, last)]


def kernel(
    n, groups,
    q_hbm, k_hbm, v_hbm, feature_hbm, inner_hbm, key_hbm, query_hbm, filter_hbm,
    first_hbm, ahead_hbm, back_hbm, last_hbm,
    out_hbm,
    q, k, v, feature, inner, key, query, first, ahead, back, last,
    tails, edge_out, edge_in, ext, sig_out, sig_in, filt_in, sig_spec, filt_spec, filt_freq, product, turned,
    conv_out, conv_in, out,
    local_sem, out_sem, edge_sem, sig_send, sig_recv, filt_send, filt_recv, share_send, share_recv,
    conv_send, conv_recv,
):
    me, part = lax.axis_index("ctx"), lax.axis_index("dp")
    right = lax.rem(me + 1, n)
    above, below = lax.rem(part + 1, groups), lax.rem(part + groups - 1, groups)
    opposite = lax.rem(part + 2, groups)
    rows = q.shape[0]
    mid, quarter = rows // 2, rows // groups

    def other(s):
        return lax.rem(me + s, n)

    def cols(g):
        return pl.ds(pl.multiple_of(g * LANES, LANES), LANES)

    def share(d):
        return pl.ds(pl.multiple_of(d * quarter, quarter), quarter)

    def arrived(ref, sem):
        pltpu.make_async_copy(ref, ref, sem).wait()

    tail = pl.ds(rows - 16, 16)
    loads = [
        pltpu.make_async_copy(src, dst, local_sem.at[at])
        for at, (src, dst) in enumerate(
            [
                (q_hbm.at[tail], tails.at[0]), (k_hbm.at[tail], tails.at[1]), (v_hbm.at[tail], tails.at[2]),
                (feature_hbm, feature),
                (k_hbm, k), (v_hbm, v), (q_hbm, q), (inner_hbm, inner), (key_hbm, key),
                (filter_hbm.at[share(part), cols(me)], filt_in.at[me, share(part)]),
                (first_hbm, first), (ahead_hbm, ahead), (back_hbm, back), (last_hbm, last), (query_hbm, query),
            ]
        )
    ]
    for load in loads[:10]:
        load.start()

    barrier = pltpu.get_barrier_semaphore()

    @pl.loop(1, n)
    def _(s):
        pl.semaphore_signal(barrier, inc=1, device_id={"ctx": other(s)}, device_id_type=MESH)

    for d in (above, below):
        pl.semaphore_signal(barrier, inc=1, device_id={"dp": d}, device_id_type=MESH)

    for load in loads[:4]:
        load.wait()

    row8 = lax.broadcasted_iota(jnp.int32, (8, LANES), 0)

    @pl.loop(0, n)
    def _(g):
        at = cols(g)
        q16, k16, v16 = (tails[stream, :, at].astype(F32) for stream in range(3))
        fk = jnp.zeros((8, LANES), F32)
        fv = jnp.zeros((8, LANES), F32)
        for lag in range(3):
            fk = fk + feature[1, pl.ds(lag, 1), at] * k16[8 - lag : 16 - lag]
            fv = fv + feature[2, pl.ds(lag, 1), at] * v16[8 - lag : 16 - lag]
        packed = jnp.where(
            row8 < 2, pltpu.roll(q16[8:], 2, 0),
            jnp.where(row8 < 4, pltpu.roll(k16[8:], 4, 0), pltpu.roll(v16[8:], 6, 0)),
        )
        edge_out[:, at] = jnp.concatenate([fk * fv, packed], axis=0).astype(BF16)

    def signal_rows(g, count):
        at = cols(g)
        feats = []
        for stream, ref in enumerate((q, k, v)):
            own = ref[pl.ds(0, count), at].astype(F32)
            ext[stream, pl.ds(8, count), :] = own
            total = feature[stream, pl.ds(0, 1), at] * own
            for lag in range(1, 3):
                total = total + feature[stream, pl.ds(lag, 1), at] * ext[stream, pl.ds(8 - lag, count), :]
            feats.append(total)
        gated = feats[1] * feats[2]
        ext[3, pl.ds(8, count), :] = gated
        total = inner[pl.ds(0, 1), at] * gated
        for lag in range(1, 7):
            total = total + inner[pl.ds(lag, 1), at] * ext[3, pl.ds(8 - lag, count), :]
        return key[pl.ds(0, count), at].astype(F32) * (feats[0] * total)

    def low(count):
        return lax.broadcasted_iota(jnp.int32, (count, LANES), 1) < LANES // 2

    def swap(a):
        return pltpu.roll(a, LANES // 2, a.ndim - 1)

    pl.semaphore_wait(barrier, n + 1)

    edge_copy = pltpu.make_async_remote_copy(
        src_ref=edge_out, dst_ref=edge_in, send_sem=edge_sem.at[0], recv_sem=edge_sem.at[1],
        device_id={"ctx": right}, device_id_type=MESH,
    )
    edge_copy.start()

    @pl.loop(1, n)
    def _(s):
        g = other(s)
        pltpu.make_async_remote_copy(
            src_ref=filter_hbm.at[share(part), cols(g)], dst_ref=filt_in.at[me, share(part)],
            send_sem=filt_send, recv_sem=filt_recv.at[me],
            device_id={"ctx": g}, device_id_type=MESH,
        ).start()

    for load in loads[10:]:
        load.start()
    for load in loads[4:9]:
        load.wait()

    def signal_send(half, at, s):
        g = other(s)
        pltpu.make_async_remote_copy(
            src_ref=sig_out.at[half, g, at], dst_ref=sig_in.at[half, me, at],
            send_sem=sig_send, recv_sem=sig_recv.at[half, me],
            device_id={"ctx": g}, device_id_type=MESH,
        ).start()

    ext[:, pl.ds(0, 8), :] = jnp.zeros((4, 8, LANES), F32)

    @pl.loop(1, n + 1)
    def _(s):
        g = other(s)
        block = signal_rows(g, rows)
        upper, lower = block[:mid], swap(block[mid:])
        sig_out[0, g] = jnp.where(low(mid), upper, lower).astype(BF16)
        sig_out[1, g] = jnp.where(low(mid), lower, upper).astype(BF16)

        @pl.when(s < n)
        def _():
            signal_send(0, pl.ds(16, mid - 16), s)

    edge_copy.wait()

    def signal_edge(g):
        edge = jnp.where(me > 0, edge_in[:, cols(g)].astype(F32), 0.0)
        for stream in range(3):
            ext[stream, pl.ds(0, 8), :] = pltpu.roll(edge[8:], 6 - 2 * stream, 0)
        ext[3, pl.ds(0, 8), :] = edge[:8]
        top = signal_rows(g, 16)
        at = pl.ds(0, 16)
        sig_out[0, g, at] = jnp.where(low(16), top, sig_out[0, g, at].astype(F32)).astype(BF16)
        sig_out[1, g, at] = jnp.where(low(16), sig_out[1, g, at].astype(F32), top).astype(BF16)

    @pl.loop(1, n)
    def _(s):
        signal_edge(other(s))
        signal_send(0, pl.ds(0, 16), s)

    signal_edge(me)
    for half in range(2):
        sig_in[half, me] = sig_out[half, me]

    @pl.loop(1, n)
    def _(s):
        g = other(s)
        arrived(filt_in.at[g, share(part)], filt_recv.at[g])

    loads[9].wait()

    def share_copy(at, to, ref):
        return pltpu.make_async_remote_copy(
            src_ref=ref, dst_ref=ref, send_sem=share_send.at[at], recv_sem=share_recv.at[at],
            device_id={"dp": to}, device_id_type=MESH,
        )

    chunks = [pl.ds(c * (n // 4), n // 4) for c in range(4)]
    shares = [share_copy(c, above, filt_in.at[chunks[c], share(part)]) for c in range(4)]
    shares += [share_copy(4 + c, below, filt_in.at[chunks[c], share(part)]) for c in range(4)]
    shares += [share_copy(8 + c, above, filt_in.at[chunks[c], share(below)]) for c in range(2)]
    shares += [share_copy(8 + c, below, filt_in.at[chunks[c], share(above)]) for c in range(2, 4)]
    for at in (0, 6, 1, 7, 2, 4, 3, 5):
        shares[at].start()

    @pl.loop(1, n)
    def _(s):
        signal_send(1, pl.ds(0, mid), s)

    for load in loads[10:]:
        load.wait()

    def first_step(source, j):
        at = [pl.ds(j * 32 + 16 * u if isinstance(j, int) else pl.multiple_of(j * 32 + 16 * u, 16), 16) for u in range(2)]
        pair = jnp.concatenate([source[:, a, :].reshape(n * 16, LANES) for a in at], axis=1)
        done = jnp.dot(first[...], pair, preferred_element_type=F32)
        return [(at[u], done[:, u * LANES : (u + 1) * LANES]) for u in range(2)]

    def filter_step(d):
        for at, done in first_step(filt_in, d):
            filt_spec[:, at, :] = done.astype(BF16).reshape(2 * n, 16, LANES)

    filter_step(part)
    for fore, rear in ((0, 2), (1, 3)):
        arrived(filt_in.at[chunks[fore], share(below)], share_recv.at[fore])
        shares[8 + fore].start()
        arrived(filt_in.at[chunks[rear], share(above)], share_recv.at[4 + rear])
        shares[8 + rear].start()
    for c in (2, 3):
        arrived(filt_in.at[chunks[c], share(below)], share_recv.at[c])
    filter_step(below)
    for c in (0, 1):
        arrived(filt_in.at[chunks[c], share(above)], share_recv.at[4 + c])
    filter_step(above)

    row = lax.broadcasted_iota(jnp.int32, (rows, LANES), 0)

    for half in range(2):
        @pl.loop(1, n)
        def _(s):
            g = other(s)
            arrived(sig_in.at[half, g], sig_recv.at[half, g])

        for j in range(mid // 32):
            for at, done in first_step(sig_in.at[half], j):
                lower = pl.ds(at.start + mid, 16)
                sig_spec[:, at, :] = done.astype(BF16).reshape(2 * n, 16, LANES)
                sig_spec[:, lower, :] = swap(done).astype(BF16).reshape(2 * n, 16, LANES)

        if half == 0:
            for c in range(4):
                arrived(filt_in.at[chunks[c], share(opposite)], share_recv.at[8 + c])
            filter_step(opposite)

        @pl.loop(0, n // UNROLL)
        def _(step):
            for u in range(UNROLL):
                p = step * UNROLL + u
                both = sig_spec[pl.ds(2 * p, 2)].reshape(2 * rows, LANES)
                if half == 0:
                    both = jnp.concatenate([both, filt_spec[pl.ds(2 * p, 2)].reshape(2 * rows, LANES)], axis=1)
                both = jnp.dot(ahead[p], both, preferred_element_type=F32)
                if half == 0:
                    both, freq = both[:, :LANES], both[:, LANES:]
                    filt_freq[p] = freq
                else:
                    freq = filt_freq[p]
                xr, hr, xi, hi = both[:rows], freq[:rows], both[rows:], freq[rows:]
                real, imag = xr * hr - xi * hi, xr * hi + xi * hr
                if u == 0:
                    alone = jnp.logical_and(row == 0, p == 0)
                    real = jnp.where(alone, xr * hr, real)
                    imag = jnp.where(alone, xi * hi, imag)
                product[p, :rows] = real.astype(BF16)
                product[p, rows:] = imag.astype(BF16)

        @pl.loop(0, n // UNROLL)
        def _(step):
            for u in range(UNROLL):
                p = step * UNROLL + u
                both = jnp.dot(back[p], product[p], preferred_element_type=F32).reshape(2, 2, mid, LANES)
                for which in range(2):
                    upper, lower = both[which, 0], swap(both[which, 1])
                    packed = jnp.where(low(mid), upper, lower) if half == 0 else jnp.where(low(mid), lower, upper)
                    turned[2 * p + which] = packed.astype(BF16)

        for j in range(mid // 32):
            at = [pl.ds(j * 32 + 16 * u, 16) for u in range(2)]
            pair = jnp.concatenate([turned[:, a, :].reshape(2 * n * 16, LANES) for a in at], axis=1)
            done = jnp.dot(last[...], pair, preferred_element_type=F32).astype(BF16)
            for u in range(2):
                conv_out[half, :, at[u], :] = done[:, u * LANES : (u + 1) * LANES].reshape(n, 16, LANES)

        @pl.loop(1, n)
        def _(s):
            g = other(s)
            pltpu.make_async_remote_copy(
                src_ref=conv_out.at[half, g], dst_ref=conv_in.at[half, me],
                send_sem=conv_send, recv_sem=conv_recv.at[half, me],
                device_id={"ctx": g}, device_id_type=MESH,
            ).start()

        conv_in[half, me] = conv_out[half, me]

    def finish(g):
        at = cols(g)
        one, two = conv_in[0, g].astype(F32), conv_in[1, g].astype(F32)
        upper = jnp.where(low(mid), one, two)
        lower = swap(jnp.where(low(mid), two, one))
        out[:mid, at] = (query[:mid, at].astype(F32) * upper).astype(BF16)
        out[mid:, at] = (query[mid:, at].astype(F32) * lower).astype(BF16)
        pltpu.make_async_copy(out.at[:, at], out_hbm.at[:, at], out_sem).start()

    finish(me)

    @pl.loop(1, n)
    def _(s):
        g = lax.rem(me + n - s, n)
        for half in range(2):
            arrived(conv_in.at[half, g], conv_recv.at[half, g])
        finish(g)

    arrived(out, out_sem)
    for sent in shares:
        sent.wait_send()
    arrived(filt_in.at[pl.ds(0, n - 1), share(part)], filt_send)
    for ref, sem in ((sig_out, sig_send), (conv_out, conv_send)):
        for half in range(2):
            arrived(ref.at[half, pl.ds(0, n - 1)], sem)


def solution(mesh):
    n, groups = mesh.shape["ctx"], mesh.shape["dp"]

    def local(se_query, se_key, se_value, feature_taps, inner_taps, li_query, li_key, long_filter):
        rows, width = se_query.shape
        tables = transform_tables(n, rows)
        dma = pltpu.SemaphoreType.DMA
        whole = pltpu.VMEM((rows, width), BF16)
        edge = pltpu.VMEM((16, width), BF16)
        halves = pltpu.VMEM((2, n, rows // 2, LANES), BF16)
        spectrum = pltpu.VMEM((2 * n, rows, LANES), BF16)
        return pl.pallas_call(
            functools.partial(kernel, n, groups),
            out_shape=jax.ShapeDtypeStruct((rows, width), BF16),
            in_specs=[pl.BlockSpec(memory_space=pl.ANY)] * 12,
            out_specs=pl.BlockSpec(memory_space=pl.ANY),
            scratch_shapes=[
                whole, whole, whole,
                pltpu.VMEM(feature_taps.shape, F32),
                pltpu.VMEM(inner_taps.shape, F32),
                whole, whole,
                *[pltpu.VMEM(t.shape, BF16) for t in tables],
                pltpu.VMEM((3, 16, width), BF16), edge, edge,
                pltpu.VMEM((4, rows + 8, LANES), F32),
                halves, halves,
                pltpu.VMEM((n, rows, LANES), BF16),
                spectrum, spectrum,
                pltpu.VMEM((n, 2 * rows, LANES), F32),
                pltpu.VMEM((n, 2 * rows, LANES), BF16),
                pltpu.VMEM((2 * n, rows // 2, LANES), BF16),
                halves, halves,
                whole,
                dma((15,)), dma, dma((2,)),
                dma, dma((2, n)),
                dma, dma((n,)),
                dma((12,)), dma((12,)),
                dma, dma((2, n)),
            ],
            compiler_params=pltpu.CompilerParams(
                collective_id=0, has_side_effects=True, vmem_limit_bytes=56 * 1024 * 1024
            ),
        )(
            se_query, se_key, se_value, feature_taps, inner_taps, li_key, li_query, long_filter,
            *[jnp.asarray(t) for t in tables],
        )

    rows_over = P(("dp", "ctx"), None)
    return jax.shard_map(
        local,
        mesh=mesh,
        in_specs=(rows_over, rows_over, rows_over, P(), P(), rows_over, rows_over, P("ctx", None)),
        out_specs=rows_over,
        check_vma=False,
    )
```

time: 62.5 us -> 53.1 us (0.85)
  Pallas kernels: 59.9 us -> 50.5 us
  other arithmetic: 2.45 us -> 0 us
  local copies, waits for them, and re-layouts: 0.01 us -> 2.29 us
    pallas_call x1, Pallas kernels: 59.9 us -> 50.5 us  [local(): pl.pallas_call(functools.partial(kernel, n, groups), out_shape=jax.ShapeD...]
    convert_element_type x1 -> x0, other arithmetic: 2.45 us -> none  [local(): return (li_query.astype(F32) * conv.astype(F32)).astype(BF16)]
    unnamed x2 -> x1, local copies, waits for them, and re-layouts: 0.01 us -> 2.29 us
where the time goes in v1:
time: 53.1 us; the launch traced here: 52.8 us
  Pallas kernels  50.5 us (95%)
  local copies, waits for them, and re-layouts  2.29 us (4%)
    pallas_call x1, Pallas kernels, local(): pl.pallas_call(functools.partial(kernel, n, groups), out_shape=jax.ShapeD...  50.5 us
    unnamed x1, local copies, waits for them, and re-layouts  2.29 us

profile of v1, /device:TPU:1, one launch (start us, length us, event | category | flops | bytes accessed | tf_op | source)
XLA Modules:
  0.0 52.8 jit_solution(12808361166600938797)
XLA Ops:
  0.0 50.5 %shard_map.118 = bf16[128,4096]{1,0:T(8,128)(2,1)} custom-call(bf16[128,4096]{1,0:T(8,128)(2,1)} %q_hbm.1, bf16[128,4096]{1,0:T(8,128)(2,1)} %k_hbm.1, bf16[128,4096]{1,0:T(8,128)(2,1)} %v_hbm.1, f32[3,3,4096]{2,1,0:T(4,128)} %feature_hbm.1, f32[7,4096]{1,0:T(8,128)} %inner_hbm.1, bf16[128,4096]{1,0:T(8,128)(2,1)} %key_hbm.1, bf16[128,4096]{1,0:T(8,128)(2,1)} %query_hbm.1, ...), custom_call_target="tpu_custom_call" | custom-call | tf_op jit(solution)/shard_map/pallas_call | solution.py:379
  50.5 2.3 %copy.14 = bf16[128,4096]{1,0:T(8,128)(2,1)} copy(bf16[128,4096]{1,0:T(8,128)(2,1)} %shard_map.118) | data formatting | bytes 2097152

commit v2 on v1

--- a/solution.py
+++ b/solution.py
@@ -14,6 +14,9 @@
 LANES = 128
 HALF = 16
 UNROLL = 16
+SIDE = 2
+SHARE = 2
+SIDES = 4
 
 
 def transform_tables(blocks, block):
@@ -61,7 +64,7 @@
     first_hbm, ahead_hbm, back_hbm, last_hbm,
     out_hbm,
     q, k, v, feature, inner, key, query, first, ahead, back, last,
-    tails, edge_out, edge_in, ext, sig_out, sig_in, filt_in, sig_spec, filt_spec, filt_freq, product, turned,
+    tails, edge_out, edge_in, ext, filt_rows, filt_out, sig_out, sig_in, filt_in, sig_spec, filt_spec, filt_freq, product, turned,
     conv_out, conv_in, out,
     local_sem, out_sem, edge_sem, sig_send, sig_recv, filt_send, filt_recv, share_send, share_recv,
     conv_send, conv_recv,
@@ -76,6 +79,15 @@
     def other(s):
         return lax.rem(me + s, n)
 
+    at_z, at_x, core = me // (2 * SIDES), me // 2 % SIDES, me % 2
+    steps = [(0, 0), (0, 1), (1, 0), (0, 3), (3, 0), (1, 1), (3, 3), (1, 3), (3, 1), (0, 2), (2, 0), (1, 2), (2, 1), (3, 2)]
+    steps += [(2, 3), (2, 2)]
+    on_z = [lax.rem(at_z + d, SIDES) * SIDES for d in range(SIDES)]
+    on_x = [lax.rem(at_x + d, SIDES) for d in range(SIDES)]
+    chips = [on_z[dz] + on_x[dx] for dz, dx in steps[::-1]]
+    peers = [2 * chip + c for chip in chips for c in (1 - core, core)][: n - 1]
+    pairs = n // 2
+
     def cols(g):
         return pl.ds(pl.multiple_of(g * LANES, LANES), LANES)
 
@@ -92,13 +104,13 @@
             [
                 (q_hbm.at[tail], tails.at[0]), (k_hbm.at[tail], tails.at[1]), (v_hbm.at[tail], tails.at[2]),
                 (feature_hbm, feature),
+                (filter_hbm.at[share(part)], filt_rows.at[0]), (filter_hbm.at[share(opposite)], filt_rows.at[1]),
                 (k_hbm, k), (v_hbm, v), (q_hbm, q), (inner_hbm, inner), (key_hbm, key),
-                (filter_hbm.at[share(part), cols(me)], filt_in.at[me, share(part)]),
                 (first_hbm, first), (ahead_hbm, ahead), (back_hbm, back), (last_hbm, last), (query_hbm, query),
             ]
         )
     ]
-    for load in loads[:10]:
+    for load in loads[:11]:
         load.start()
 
     barrier = pltpu.get_barrier_semaphore()
@@ -112,6 +124,16 @@
 
     for load in loads[:4]:
         load.wait()
+
+    def low(count):
+        return lax.broadcasted_iota(jnp.int32, (count, LANES), 1) < LANES // 2
+
+    def swap(a):
+        return pltpu.roll(a, LANES // 2, a.ndim - 1)
+
+    def spread(upper, lower, half):
+        near, far = (upper, lower) if half == 0 else (lower, upper)
+        return jnp.where(low(mid), near, swap(far)), jnp.where(low(mid), swap(near), far)
 
     row8 = lax.broadcasted_iota(jnp.int32, (8, LANES), 0)
 
@@ -130,7 +152,7 @@
         )
         edge_out[:, at] = jnp.concatenate([fk * fv, packed], axis=0).astype(BF16)
 
-    def signal_rows(g, count):
+    def signal_rows(g, count, ext):
         at = cols(g)
         feats = []
         for stream, ref in enumerate((q, k, v)):
@@ -147,11 +169,19 @@
             total = total + inner[pl.ds(lag, 1), at] * ext[3, pl.ds(8 - lag, count), :]
         return key[pl.ds(0, count), at].astype(F32) * (feats[0] * total)
 
-    def low(count):
-        return lax.broadcasted_iota(jnp.int32, (count, LANES), 1) < LANES // 2
-
-    def swap(a):
-        return pltpu.roll(a, LANES // 2, a.ndim - 1)
+    quarters = (part, opposite)
+    for which in range(2):
+        loads[4 + which].wait()
+
+    @pl.loop(0, pairs)
+    def _(j):
+        for which in range(2):
+            one, two = (filt_rows[which, :, cols(b)].astype(F32) for b in (j, pairs + j))
+            filt_out[which, 2 * j] = jnp.where(low(quarter), one, swap(two)).astype(BF16)
+            filt_out[which, 2 * j + 1] = jnp.where(low(quarter), swap(one), two).astype(BF16)
+
+    for which in range(2):
+        filt_in[me, share(quarters[which]), :] = filt_out[which, me]
 
     pl.semaphore_wait(barrier, n + 1)
 
@@ -161,89 +191,87 @@
     )
     edge_copy.start()
 
-    @pl.loop(1, n)
-    def _(s):
-        g = other(s)
-        pltpu.make_async_remote_copy(
-            src_ref=filter_hbm.at[share(part), cols(g)], dst_ref=filt_in.at[me, share(part)],
-            send_sem=filt_send, recv_sem=filt_recv.at[me],
+    def filter_copy(which, g):
+        return pltpu.make_async_remote_copy(
+            src_ref=filt_out.at[which, g], dst_ref=filt_in.at[me, share(quarters[which])],
+            send_sem=filt_send.at[which], recv_sem=filt_recv.at[which, me],
             device_id={"ctx": g}, device_id_type=MESH,
-        ).start()
-
-    for load in loads[10:]:
+        )
+
+    for g in peers:
+        filter_copy(0, g).start()
+
+    for load in loads[11:]:
         load.start()
-    for load in loads[4:9]:
+    for load in loads[6:11]:
         load.wait()
 
-    def signal_send(half, at, s):
-        g = other(s)
-        pltpu.make_async_remote_copy(
-            src_ref=sig_out.at[half, g, at], dst_ref=sig_in.at[half, me, at],
-            send_sem=sig_send, recv_sem=sig_recv.at[half, me],
+    def signal_copy(half, g):
+        return pltpu.make_async_remote_copy(
+            src_ref=sig_out.at[half, g], dst_ref=sig_in.at[half, me],
+            send_sem=sig_send.at[half], recv_sem=sig_recv.at[half, me],
             device_id={"ctx": g}, device_id_type=MESH,
-        ).start()
-
-    ext[:, pl.ds(0, 8), :] = jnp.zeros((4, 8, LANES), F32)
-
-    @pl.loop(1, n + 1)
-    def _(s):
-        g = other(s)
-        block = signal_rows(g, rows)
-        upper, lower = block[:mid], swap(block[mid:])
-        sig_out[0, g] = jnp.where(low(mid), upper, lower).astype(BF16)
-        sig_out[1, g] = jnp.where(low(mid), lower, upper).astype(BF16)
-
-        @pl.when(s < n)
-        def _():
-            signal_send(0, pl.ds(16, mid - 16), s)
-
-    edge_copy.wait()
-
-    def signal_edge(g):
-        edge = jnp.where(me > 0, edge_in[:, cols(g)].astype(F32), 0.0)
+        )
+
+    def signal_pair(half, j, ext):
+        block = half * pairs + j
+        edge = jnp.where(me > 0, edge_in[:, cols(block)].astype(F32), 0.0)
         for stream in range(3):
             ext[stream, pl.ds(0, 8), :] = pltpu.roll(edge[8:], 6 - 2 * stream, 0)
         ext[3, pl.ds(0, 8), :] = edge[:8]
-        top = signal_rows(g, 16)
-        at = pl.ds(0, 16)
-        sig_out[0, g, at] = jnp.where(low(16), top, sig_out[0, g, at].astype(F32)).astype(BF16)
-        sig_out[1, g, at] = jnp.where(low(16), sig_out[1, g, at].astype(F32), top).astype(BF16)
+        rows_of = signal_rows(block, rows, ext)
+        for c, packed in enumerate(spread(rows_of[:mid], rows_of[mid:], half)):
+            sig_out[half, 2 * j + c] = packed.astype(BF16)
+
+    edge_copy.wait()
+
+    def chip(e):
+        place = chips[0]
+        for at in range(1, pairs):
+            place = jnp.where(e == at, chips[at], place)
+        return place
+
+    @pl.loop(0, pairs - SIDE, step=SIDE)
+    def _(e):
+        places = [chip(e + u) for u in range(SIDE)]
+        for u in range(SIDE):
+            signal_pair(0, places[u], ext.at[u])
+        for j in places:
+            for c in range(2):
+                signal_copy(0, 2 * j + c).start()
+
+    for u in range(SIDE):
+        signal_pair(0, chips[pairs - SIDE + u], ext.at[u])
+    for g in peers[2 * (pairs - SIDE) :]:
+        signal_copy(0, g).start()
+    sig_in[0, me] = sig_out[0, me]
 
     @pl.loop(1, n)
     def _(s):
-        signal_edge(other(s))
-        signal_send(0, pl.ds(0, 16), s)
-
-    signal_edge(me)
-    for half in range(2):
-        sig_in[half, me] = sig_out[half, me]
-
-    @pl.loop(1, n)
-    def _(s):
-        g = other(s)
-        arrived(filt_in.at[g, share(part)], filt_recv.at[g])
-
-    loads[9].wait()
-
-    def share_copy(at, to, ref):
+        arrived(filt_in.at[other(s), share(part)], filt_recv.at[0, other(s)])
+
+    def share_copy(at, to, piece):
+        ref = filt_in.at[pl.ds(piece * SHARE, SHARE), share(part)]
         return pltpu.make_async_remote_copy(
             src_ref=ref, dst_ref=ref, send_sem=share_send.at[at], recv_sem=share_recv.at[at],
             device_id={"dp": to}, device_id_type=MESH,
         )
 
-    chunks = [pl.ds(c * (n // 4), n // 4) for c in range(4)]
-    shares = [share_copy(c, above, filt_in.at[chunks[c], share(part)]) for c in range(4)]
-    shares += [share_copy(4 + c, below, filt_in.at[chunks[c], share(part)]) for c in range(4)]
-    shares += [share_copy(8 + c, above, filt_in.at[chunks[c], share(below)]) for c in range(2)]
-    shares += [share_copy(8 + c, below, filt_in.at[chunks[c], share(above)]) for c in range(2, 4)]
-    for at in (0, 6, 1, 7, 2, 4, 3, 5):
-        shares[at].start()
-
-    @pl.loop(1, n)
-    def _(s):
-        signal_send(1, pl.ds(0, mid), s)
-
-    for load in loads[10:]:
+    for piece in range(n // SHARE):
+        for at, to in enumerate((above, below)):
+            share_copy(at, to, piece).start()
+
+    for g in peers:
+        filter_copy(1, g).start()
+
+    @pl.loop(0, pairs, step=SIDE)
+    def _(j):
+        for u in range(SIDE):
+            signal_pair(1, j + u, ext.at[u])
+
+    sig_in[1, me] = sig_out[1, me]
+
+    for load in loads[11:]:
         load.wait()
 
     def first_step(source, j):
@@ -257,17 +285,10 @@
             filt_spec[:, at, :] = done.astype(BF16).reshape(2 * n, 16, LANES)
 
     filter_step(part)
-    for fore, rear in ((0, 2), (1, 3)):
-        arrived(filt_in.at[chunks[fore], share(below)], share_recv.at[fore])
-        shares[8 + fore].start()
-        arrived(filt_in.at[chunks[rear], share(above)], share_recv.at[4 + rear])
-        shares[8 + rear].start()
-    for c in (2, 3):
-        arrived(filt_in.at[chunks[c], share(below)], share_recv.at[c])
-    filter_step(below)
-    for c in (0, 1):
-        arrived(filt_in.at[chunks[c], share(above)], share_recv.at[4 + c])
-    filter_step(above)
+    arrived(sig_out.at[0, pl.ds(0, n - 1)], sig_send.at[0])
+    arrived(filt_out.at[1, pl.ds(0, n - 1)], filt_send.at[1])
+    for g in peers:
+        signal_copy(1, g).start()
 
     row = lax.broadcasted_iota(jnp.int32, (rows, LANES), 0)
 
@@ -284,8 +305,14 @@
                 sig_spec[:, lower, :] = swap(done).astype(BF16).reshape(2 * n, 16, LANES)
 
         if half == 0:
-            for c in range(4):
-                arrived(filt_in.at[chunks[c], share(opposite)], share_recv.at[8 + c])
+            for at, d in enumerate((below, above)):
+                arrived(filt_in.at[:, share(d)], share_recv.at[at])
+                filter_step(d)
+
+            @pl.loop(1, n)
+            def _(s):
+                arrived(filt_in.at[other(s), share(opposite)], filt_recv.at[1, other(s)])
+
             filter_step(opposite)
 
         @pl.loop(0, n // UNROLL)
@@ -327,42 +354,43 @@
             for u in range(2):
                 conv_out[half, :, at[u], :] = done[:, u * LANES : (u + 1) * LANES].reshape(n, 16, LANES)
 
-        @pl.loop(1, n)
-        def _(s):
-            g = other(s)
+        for g in peers:
             pltpu.make_async_remote_copy(
                 src_ref=conv_out.at[half, g], dst_ref=conv_in.at[half, me],
-                send_sem=conv_send, recv_sem=conv_recv.at[half, me],
+                send_sem=conv_send.at[half], recv_sem=conv_recv.at[half, me],
                 device_id={"ctx": g}, device_id_type=MESH,
             ).start()
 
         conv_in[half, me] = conv_out[half, me]
 
-    def finish(g):
-        at = cols(g)
-        one, two = conv_in[0, g].astype(F32), conv_in[1, g].astype(F32)
-        upper = jnp.where(low(mid), one, two)
-        lower = swap(jnp.where(low(mid), two, one))
+    def finish(half, j):
+        at = cols(half * pairs + j)
+        one, two = (conv_in[half, 2 * j + c].astype(F32) for c in range(2))
+        upper, lower = jnp.where(low(mid), one, swap(two)), jnp.where(low(mid), swap(one), two)
+        if half == 1:
+            upper, lower = lower, upper
         out[:mid, at] = (query[:mid, at].astype(F32) * upper).astype(BF16)
         out[mid:, at] = (query[mid:, at].astype(F32) * lower).astype(BF16)
         pltpu.make_async_copy(out.at[:, at], out_hbm.at[:, at], out_sem).start()
 
-    finish(me)
-
-    @pl.loop(1, n)
-    def _(s):
-        g = lax.rem(me + n - s, n)
-        for half in range(2):
-            arrived(conv_in.at[half, g], conv_recv.at[half, g])
-        finish(g)
+    for half in range(2):
+        @pl.loop(1, n)
+        def _(s):
+            arrived(conv_in.at[half, other(s)], conv_recv.at[half, other(s)])
+
+        @pl.loop(0, pairs, step=4)
+        def _(j):
+            for u in range(4):
+                finish(half, j + u)
 
     arrived(out, out_sem)
-    for sent in shares:
-        sent.wait_send()
-    arrived(filt_in.at[pl.ds(0, n - 1), share(part)], filt_send)
-    for ref, sem in ((sig_out, sig_send), (conv_out, conv_send)):
-        for half in range(2):
-            arrived(ref.at[half, pl.ds(0, n - 1)], sem)
+    for at in range(2):
+        arrived(filt_in.at[:, share(part)], share_send.at[at])
+
+    arrived(sig_out.at[1, pl.ds(0, n - 1)], sig_send.at[1])
+    arrived(filt_out.at[0, pl.ds(0, n - 1)], filt_send.at[0])
+    for half in range(2):
+        arrived(conv_out.at[half, pl.ds(0, n - 1)], conv_send.at[half])
 
 
 def solution(mesh):
@@ -388,7 +416,9 @@
                 whole, whole,
                 *[pltpu.VMEM(t.shape, BF16) for t in tables],
                 pltpu.VMEM((3, 16, width), BF16), edge, edge,
-                pltpu.VMEM((4, rows + 8, LANES), F32),
+                pltpu.VMEM((SIDE, 4, rows + 8, LANES), F32),
+                pltpu.VMEM((2, rows // groups, width), BF16),
+                pltpu.VMEM((2, n, rows // groups, LANES), BF16),
                 halves, halves,
                 pltpu.VMEM((n, rows, LANES), BF16),
                 spectrum, spectrum,
@@ -397,11 +427,11 @@
                 pltpu.VMEM((2 * n, rows // 2, LANES), BF16),
                 halves, halves,
                 whole,
-                dma((15,)), dma, dma((2,)),
-                dma, dma((2, n)),
-                dma, dma((n,)),
-                dma((12,)), dma((12,)),
-                dma, dma((2, n)),
+                dma((16,)), dma, dma((2,)),
+                dma((2,)), dma((2, n)),
+                dma((2,)), dma((2, n)),
+                dma((2,)), dma((2,)),
+                dma((2,)), dma((2, n)),
             ],
             compiler_params=pltpu.CompilerParams(
                 collective_id=0, has_side_effects=True, vmem_limit_bytes=56 * 1024 * 1024

time: 53.1 us -> 49.8 us (0.938)
  Pallas kernels: 50.5 us -> 47.3 us
    pallas_call x1, Pallas kernels: 50.5 us -> 47.3 us  [local(): pl.pallas_call(functools.partial(kernel, n, groups), out_shape=jax.ShapeD...]
where the time goes in v2:
time: 49.8 us; the launch traced here: 49.6 us
  Pallas kernels  47.3 us (95%)
  local copies, waits for them, and re-layouts  2.29 us (5%)
    pallas_call x1, Pallas kernels, local(): pl.pallas_call(functools.partial(kernel, n, groups), out_shape=jax.ShapeD...  47.3 us
    unnamed x1, local copies, waits for them, and re-layouts  2.29 us

profile of v2, /device:TPU:1, one launch (start us, length us, event | category | flops | bytes accessed | tf_op | source)
XLA Modules:
  0.0 49.6 jit_solution(6505036521750529063)
XLA Ops:
  0.0 47.3 %shard_map.118 = bf16[128,4096]{1,0:T(8,128)(2,1)} custom-call(bf16[128,4096]{1,0:T(8,128)(2,1)} %q_hbm.1, bf16[128,4096]{1,0:T(8,128)(2,1)} %k_hbm.1, bf16[128,4096]{1,0:T(8,128)(2,1)} %v_hbm.1, f32[3,3,4096]{2,1,0:T(4,128)} %feature_hbm.1, f32[7,4096]{1,0:T(8,128)} %inner_hbm.1, bf16[128,4096]{1,0:T(8,128)(2,1)} %key_hbm.1, bf16[128,4096]{1,0:T(8,128)(2,1)} %query_hbm.1, ...), custom_call_target="tpu_custom_call" | custom-call | tf_op jit(solution)/shard_map/pallas_call | solution.py:407
  47.3 2.3 %copy.14 = bf16[128,4096]{1,0:T(8,128)(2,1)} copy(bf16[128,4096]{1,0:T(8,128)(2,1)} %shard_map.118) | data formatting | bytes 2097152

commit v3 on v2

--- a/solution.py
+++ b/solution.py
@@ -13,7 +13,7 @@
 F32, BF16 = jnp.float32, jnp.bfloat16
 LANES = 128
 HALF = 16
-UNROLL = 16
+UNROLL = 32
 SIDE = 2
 SHARE = 2
 SIDES = 4
@@ -62,11 +62,11 @@
     n, groups,
     q_hbm, k_hbm, v_hbm, feature_hbm, inner_hbm, key_hbm, query_hbm, filter_hbm,
     first_hbm, ahead_hbm, back_hbm, last_hbm,
-    out_hbm,
+    out,
     q, k, v, feature, inner, key, query, first, ahead, back, last,
     tails, edge_out, edge_in, ext, filt_rows, filt_out, sig_out, sig_in, filt_in, sig_spec, filt_spec, filt_freq, product, turned,
-    conv_out, conv_in, out,
-    local_sem, out_sem, edge_sem, sig_send, sig_recv, filt_send, filt_recv, share_send, share_recv,
+    conv_out, conv_in,
+    local_sem, edge_sem, sig_send, sig_recv, filt_send, filt_recv, share_send, share_recv,
     conv_send, conv_recv,
 ):
     me, part = lax.axis_index("ctx"), lax.axis_index("dp")
@@ -371,19 +371,14 @@
             upper, lower = lower, upper
         out[:mid, at] = (query[:mid, at].astype(F32) * upper).astype(BF16)
         out[mid:, at] = (query[mid:, at].astype(F32) * lower).astype(BF16)
-        pltpu.make_async_copy(out.at[:, at], out_hbm.at[:, at], out_sem).start()
 
     for half in range(2):
-        @pl.loop(1, n)
-        def _(s):
-            arrived(conv_in.at[half, other(s)], conv_recv.at[half, other(s)])
-
-        @pl.loop(0, pairs, step=4)
-        def _(j):
-            for u in range(4):
-                finish(half, j + u)
-
-    arrived(out, out_sem)
+        for e in range(0, pairs, 4):
+            for at in range(2 * e, min(2 * e + 8, n - 1)):
+                arrived(conv_in.at[half, peers[at]], conv_recv.at[half, peers[at]])
+            for j in chips[e : e + 4]:
+                finish(half, j)
+
     for at in range(2):
         arrived(filt_in.at[:, share(part)], share_send.at[at])
 
@@ -406,9 +401,9 @@
         spectrum = pltpu.VMEM((2 * n, rows, LANES), BF16)
         return pl.pallas_call(
             functools.partial(kernel, n, groups),
-            out_shape=jax.ShapeDtypeStruct((rows, width), BF16),
+            out_shape=pltpu.VMEM((rows, width), BF16),
             in_specs=[pl.BlockSpec(memory_space=pl.ANY)] * 12,
-            out_specs=pl.BlockSpec(memory_space=pl.ANY),
+            out_specs=pl.BlockSpec(memory_space=pltpu.VMEM),
             scratch_shapes=[
                 whole, whole, whole,
                 pltpu.VMEM(feature_taps.shape, F32),
@@ -426,8 +421,7 @@
                 pltpu.VMEM((n, 2 * rows, LANES), BF16),
                 pltpu.VMEM((2 * n, rows // 2, LANES), BF16),
                 halves, halves,
-                whole,
-                dma((16,)), dma, dma((2,)),
+                dma((16,)), dma((2,)),
                 dma((2,)), dma((2, n)),
                 dma((2,)), dma((2, n)),
                 dma((2,)), dma((2,)),

time: 49.8 us -> 46.6 us (0.936)
  Pallas kernels: 47.3 us -> 45.5 us
  local copies, waits for them, and re-layouts: 2.29 us -> 0.97 us
    pallas_call x1, Pallas kernels: 47.3 us -> 45.5 us  [local(): pl.pallas_call(functools.partial(kernel, n, groups), out_shape=pltpu.VMEM...]
    unnamed x1, local copies, waits for them, and re-layouts: 2.29 us -> 0.97 us
where the time goes in v3:
time: 46.6 us; the launch traced here: 46.5 us
  Pallas kernels  45.5 us (98%)
  local copies, waits for them, and re-layouts  0.97 us (2%)
    pallas_call x1, Pallas kernels, local(): pl.pallas_call(functools.partial(kernel, n, groups), out_shape=pltpu.VMEM...  45.5 us
    unnamed x1, local copies, waits for them, and re-layouts  0.97 us

profile of v3, /device:TPU:1, one launch (start us, length us, event | category | flops | bytes accessed | tf_op | source)
XLA Modules:
  0.0 46.5 jit_solution(1632871485358885324)
XLA Ops:
  0.0 45.5 %shard_map.118 = bf16[128,4096]{1,0:T(8,128)(2,1)S(1)} custom-call(bf16[128,4096]{1,0:T(8,128)(2,1)} %q_hbm.1, bf16[128,4096]{1,0:T(8,128)(2,1)} %k_hbm.1, bf16[128,4096]{1,0:T(8,128)(2,1)} %v_hbm.1, f32[3,3,4096]{2,1,0:T(4,128)} %feature_hbm.1, f32[7,4096]{1,0:T(8,128)} %inner_hbm.1, bf16[128,4096]{1,0:T(8,128)(2,1)} %key_hbm.1, ...), custom_call_target="tpu_custom_call" | custom-call | tf_op jit(solution)/shard_map/pallas_call | solution.py:402
  45.5 1.0 %copy.14 = bf16[128,4096]{1,0:T(8,128)(2,1)} copy(bf16[128,4096]{1,0:T(8,128)(2,1)S(1)} %shard_map.118) | data formatting | bytes 2097152

commit v4 on v3

--- a/solution.py
+++ b/solution.py
@@ -213,15 +213,34 @@
             device_id={"ctx": g}, device_id_type=MESH,
         )
 
-    def signal_pair(half, j, ext):
-        block = half * pairs + j
+    def signal_edge(block, ext):
         edge = jnp.where(me > 0, edge_in[:, cols(block)].astype(F32), 0.0)
         for stream in range(3):
             ext[stream, pl.ds(0, 8), :] = pltpu.roll(edge[8:], 6 - 2 * stream, 0)
         ext[3, pl.ds(0, 8), :] = edge[:8]
+
+    def signal_top(j, ext):
+        signal_edge(j, ext)
+        top = signal_rows(j, 16, ext)
+        at = pl.ds(0, 16)
+        sig_out[0, 2 * j, at] = jnp.where(low(16), top, sig_out[0, 2 * j, at].astype(F32)).astype(BF16)
+        sig_out[0, 2 * j + 1, at] = jnp.where(low(16), swap(top), sig_out[0, 2 * j + 1, at].astype(F32)).astype(BF16)
+
+    def signal_pair(half, j, ext):
+        block = half * pairs + j
+        if half == 1:
+            signal_edge(block, ext)
         rows_of = signal_rows(block, rows, ext)
         for c, packed in enumerate(spread(rows_of[:mid], rows_of[mid:], half)):
             sig_out[half, 2 * j + c] = packed.astype(BF16)
+
+    for u in range(SIDE):
+        ext[u, :, pl.ds(0, 8), :] = jnp.zeros((4, 8, LANES), F32)
+
+    @pl.loop(0, pairs, step=SIDE)
+    def _(j):
+        for u in range(SIDE):
+            signal_pair(0, j + u, ext.at[u])
 
     edge_copy.wait()
 
@@ -235,13 +254,13 @@
     def _(e):
         places = [chip(e + u) for u in range(SIDE)]
         for u in range(SIDE):
-            signal_pair(0, places[u], ext.at[u])
+            signal_top(places[u], ext.at[u])
         for j in places:
             for c in range(2):
                 signal_copy(0, 2 * j + c).start()
 
     for u in range(SIDE):
-        signal_pair(0, chips[pairs - SIDE + u], ext.at[u])
+        signal_top(chips[pairs - SIDE + u], ext.at[u])
     for g in peers[2 * (pairs - SIDE) :]:
         signal_copy(0, g).start()
     sig_in[0, me] = sig_out[0, me]

time: 46.6 us -> 45.9 us (0.985)
  Pallas kernels: 45.5 us -> 44.8 us
    pallas_call x1, Pallas kernels: 45.5 us -> 44.8 us  [local(): pl.pallas_call(functools.partial(kernel, n, groups), out_shape=pltpu.VMEM...]
where the time goes in v4:
time: 45.9 us; the launch traced here: 45.8 us
  Pallas kernels  44.8 us (98%)
  local copies, waits for them, and re-layouts  0.97 us (2%)
    pallas_call x1, Pallas kernels, local(): pl.pallas_call(functools.partial(kernel, n, groups), out_shape=pltpu.VMEM...  44.8 us
    unnamed x1, local copies, waits for them, and re-layouts  0.97 us

profile of v4, /device:TPU:1, one launch (start us, length us, event | category | flops | bytes accessed | tf_op | source)
XLA Modules:
  0.0 45.8 jit_solution(6810755261306322024)
XLA Ops:
  0.0 44.8 %shard_map.118 = bf16[128,4096]{1,0:T(8,128)(2,1)S(1)} custom-call(bf16[128,4096]{1,0:T(8,128)(2,1)} %q_hbm.1, bf16[128,4096]{1,0:T(8,128)(2,1)} %k_hbm.1, bf16[128,4096]{1,0:T(8,128)(2,1)} %v_hbm.1, f32[3,3,4096]{2,1,0:T(4,128)} %feature_hbm.1, f32[7,4096]{1,0:T(8,128)} %inner_hbm.1, bf16[128,4096]{1,0:T(8,128)(2,1)} %key_hbm.1, ...), custom_call_target="tpu_custom_call" | custom-call | tf_op jit(solution)/shard_map/pallas_call | solution.py:421
  44.8 1.0 %copy.14 = bf16[128,4096]{1,0:T(8,128)(2,1)} copy(bf16[128,4096]{1,0:T(8,128)(2,1)S(1)} %shard_map.118) | data formatting | bytes 2097152

commit v5 on v4

--- a/solution.py
+++ b/solution.py
@@ -110,7 +110,7 @@
             ]
         )
     ]
-    for load in loads[:11]:
+    for load in loads[:6]:
         load.start()
 
     barrier = pltpu.get_barrier_semaphore()
@@ -122,6 +122,8 @@
     for d in (above, below):
         pl.semaphore_signal(barrier, inc=1, device_id={"dp": d}, device_id_type=MESH)
 
+    for load in loads[6:11]:
+        load.start()
     for load in loads[:4]:
         load.wait()
 
@@ -137,8 +139,7 @@
 
     row8 = lax.broadcasted_iota(jnp.int32, (8, LANES), 0)
 
-    @pl.loop(0, n)
-    def _(g):
+    def pack_edge(g):
         at = cols(g)
         q16, k16, v16 = (tails[stream, :, at].astype(F32) for stream in range(3))
         fk = jnp.zeros((8, LANES), F32)
@@ -151,6 +152,11 @@
             jnp.where(row8 < 4, pltpu.roll(k16[8:], 4, 0), pltpu.roll(v16[8:], 6, 0)),
         )
         edge_out[:, at] = jnp.concatenate([fk * fv, packed], axis=0).astype(BF16)
+
+    @pl.loop(0, n, step=4)
+    def _(g):
+        for u in range(4):
+            pack_edge(g + u)
 
     def signal_rows(g, count, ext):
         at = cols(g)
@@ -173,12 +179,16 @@
     for which in range(2):
         loads[4 + which].wait()
 
-    @pl.loop(0, pairs)
-    def _(j):
+    def regroup(j):
         for which in range(2):
             one, two = (filt_rows[which, :, cols(b)].astype(F32) for b in (j, pairs + j))
             filt_out[which, 2 * j] = jnp.where(low(quarter), one, swap(two)).astype(BF16)
             filt_out[which, 2 * j + 1] = jnp.where(low(quarter), swap(one), two).astype(BF16)
+
+    @pl.loop(0, pairs, step=4)
+    def _(j):
+        for u in range(4):
+            regroup(j + u)
 
     for which in range(2):
         filt_in[me, share(quarters[which]), :] = filt_out[which, me]

time: 45.9 us -> 45.7 us (level)
  no operation moved by 1% of the time
where the time goes in v5:
time: 45.7 us; the launch traced here: 45.6 us
  Pallas kernels  44.6 us (98%)
  local copies, waits for them, and re-layouts  0.97 us (2%)
    pallas_call x1, Pallas kernels, local(): pl.pallas_call(functools.partial(kernel, n, groups), out_shape=pltpu.VMEM...  44.6 us
    unnamed x1, local copies, waits for them, and re-layouts  0.97 us

profile of v5, /device:TPU:1, one launch (start us, length us, event | category | flops | bytes accessed | tf_op | source)
XLA Modules:
  0.0 45.6 jit_solution(9304728612986647290)
XLA Ops:
  0.0 44.6 %shard_map.118 = bf16[128,4096]{1,0:T(8,128)(2,1)S(1)} custom-call(bf16[128,4096]{1,0:T(8,128)(2,1)} %q_hbm.1, bf16[128,4096]{1,0:T(8,128)(2,1)} %k_hbm.1, bf16[128,4096]{1,0:T(8,128)(2,1)} %v_hbm.1, f32[3,3,4096]{2,1,0:T(4,128)} %feature_hbm.1, f32[7,4096]{1,0:T(8,128)} %inner_hbm.1, bf16[128,4096]{1,0:T(8,128)(2,1)} %key_hbm.1, ...), custom_call_target="tpu_custom_call" | custom-call | tf_op jit(solution)/shard_map/pallas_call | solution.py:431
  44.6 1.0 %copy.14 = bf16[128,4096]{1,0:T(8,128)(2,1)} copy(bf16[128,4096]{1,0:T(8,128)(2,1)S(1)} %shard_map.118) | data formatting | bytes 2097152
